TPU v7x, 32 devices: a whole 2x2x4 slice. The times are simulated.
32 devices in a mesh: cx: 4 (over z), cy: 8 (over y, x, core).
Axes of the slice: x: 2, y: 2, z: 4, core: 2. Of those that a mesh axis runs over, the one named last changes fastest.
Arguments:
- points_block: bfloat16 [256, 64, 256], P(('cx', 'cy')), may hold values from -6 to 6
- leaf_basis: bfloat16 [256, 64, 256], P(('cx', 'cy')), may hold values from -0.375 to 0.375
- near_blocks: bfloat16 [256, 4, 256, 256], P(('cx', 'cy')), may hold values from -0.1875 to 0.1875
- near_ids: int32 [256, 4], P(('cx', 'cy')), may hold values from 0 to 255, as said below
- local_transfer: bfloat16 [224, 128, 64], P(('cx', 'cy')), may hold values from -0.5 to 0.5
- far_coupling: bfloat16 [256, 8, 64, 64], P(('cx', 'cy')), may hold values from -0.25 to 0.25
- far_ids: int32 [256, 8], P(('cx', 'cy')), may hold values from 0 to 255, as said below
- upper_transfer: bfloat16 [31, 128, 64], replicated, may hold values from -0.5 to 0.5
- upper_coupling: bfloat16 [31, 64, 64], replicated, may hold values from -0.75 to 0.75
Outputs:
- product: bfloat16 [256, 64, 256], P(('cx', 'cy'))
Inputs may be any that keep to these rules, and one draw needn't show every extreme that they name: `near_ids`: slot 0 of each leaf is the leaf itself; every id names a leaf of the same device or of the two devices before or after it, devices numbered in the order cx then cy. `far_ids`: every id names a leaf of the same device or of the two devices before or after it, devices numbered in the order cx then cy.
All inputs are finite; a program needn't handle non-finite values.
Results may differ from a plain program's by a relative error of at most 0.004.
Values may be sent and summed in bfloat16 or wider, within the bound.
A program may use at most 128 MiB of HBM per device.

v0:
```python
import functools

import jax
import jax.numpy as jnp
from jax import lax
from jax.experimental import pallas as pl
from jax.experimental.pallas import tpu as pltpu
from jax.sharding import PartitionSpec as P

F32 = jnp.float32
BF16 = jnp.bfloat16
CHUNKS = 2
REACH = 2


def levels_of(count):
    return count.bit_length() - 1


def kernel(
    n_cx,
    n_cy,
    near_ids,
    far_ids,
    points,
    basis,
    near,
    local_transfer,
    far,
    upper_transfer,
    upper_coupling,
    out,
    win_cols,
    win_skel,
    basis_v,
    near_v,
    local_v,
    far_v,
    upper_v,
    coup_v,
    acc,
    leaf_pairs,
    group,
    roots,
    load_sem,
    cols_send,
    cols_recv,
    mate_send,
    mate_recv,
    relay_send,
    relay_recv,
    skel_send,
    skel_recv,
    group_send,
    group_recv,
    root_send,
    root_recv,
):
    leaves, cols, leaf = points.shape
    rank = basis.shape[1]
    knear, kfar = near.shape[1], far.shape[1]
    n = n_cx * n_cy
    cx, cy = lax.axis_index("cx"), lax.axis_index("cy")
    me = cx * n_cy + cy
    odd = lax.rem(me, 2)
    mate = me + 1 - 2 * odd
    up_group, up_all = levels_of(n_cy), levels_of(n)

    def at(position):
        return (lax.div(position, n_cy), lax.rem(position, n_cy))

    loads = []

    def load(src, dst):
        copy = pltpu.make_async_copy(src, dst, load_sem.at[len(loads)])
        copy.start()
        loads.append(copy)
        return copy

    own = pl.ds(REACH * leaves, leaves)
    get_points = load(points, win_cols.at[own])
    get_basis = load(basis, basis_v)
    get_local = load(local_transfer, local_v)
    get_upper = []
    offset, kept = 0, 0
    starts = []
    for level in range(1, up_all):
        width = n >> level
        here = max(n_cy >> level, 1) if level <= up_group else width
        first = offset + (cx * here if level <= up_group else 0)
        starts.append(kept)
        get_upper.append(
            load(upper_transfer.at[pl.ds(first, here)], upper_v.at[pl.ds(kept, here)])
        )
        kept += here
        offset += width
    get_coup = []
    offset = 0
    for level in range(1, up_all + 1):
        row = offset + lax.div(me, 1 << level)
        get_coup.append(load(upper_coupling.at[row], coup_v.at[level - 1]))
        offset += n >> level
    get_near = load(near, near_v)
    get_far = load(far, far_v)

    barrier = pltpu.get_barrier_semaphore()
    for j in range(1, n_cy):
        pl.semaphore_signal(
            barrier, inc=1, device_id=(cx, lax.rem(cy + j, n_cy)), device_id_type=pl.DeviceIdType.MESH
        )
    for j in range(1, n_cx):
        pl.semaphore_signal(
            barrier, inc=1, device_id=(lax.rem(cx + j, n_cx), cy), device_id_type=pl.DeviceIdType.MESH
        )

    def exists(by):
        return me >= -by if by < 0 else me + by < n

    def outside(by):
        edge = cy < -by if by < 0 else cy + by >= n_cy
        return jnp.logical_and(exists(by), edge)

    offsets = (2, -2, 1, -1)
    for by in offsets:

        @pl.when(outside(by))
        def _(by=by):
            pl.semaphore_signal(
                barrier, inc=1, device_id=at(me + by), device_id_type=pl.DeviceIdType.MESH
            )

    peers = n_cy - 1 + n_cx - 1
    for by in offsets:
        peers = peers + jnp.where(outside(by), 1, 0)
    pl.semaphore_wait(barrier, peers)

    def remote(src, dst, send, recv, target):
        return pltpu.make_async_remote_copy(
            src_ref=src,
            dst_ref=dst,
            send_sem=send,
            recv_sem=recv,
            device_id=target,
            device_id_type=pl.DeviceIdType.MESH,
        )

    size = leaves // CHUNKS

    def piece(slot, chunk):
        return win_cols.at[pl.ds(slot * leaves + chunk * size, size)]

    def cols_copy(which, chunk):
        by = (2, -2)[which]
        return remote(
            piece(REACH, chunk),
            piece(REACH - by, chunk),
            cols_send.at[which, chunk],
            cols_recv.at[which, chunk],
            at(me + by),
        )

    mate_copy = remote(
        win_cols.at[own],
        win_cols.at[pl.ds((REACH - 1 + 2 * odd) * leaves, leaves)],
        mate_send,
        mate_recv,
        at(mate),
    )

    def relay_copy(chunk):
        return remote(
            piece(4 - 4 * odd, chunk),
            piece(3 - 2 * odd, chunk),
            relay_send.at[chunk],
            relay_recv.at[chunk],
            at(mate),
        )

    get_points.wait()
    for chunk in range(CHUNKS):
        for which, by in enumerate((2, -2)):

            @pl.when(exists(by))
            def _(which=which, chunk=chunk):
                cols_copy(which, chunk).start()

    mate_copy.start()

    lane = lax.broadcasted_iota(jnp.int32, (rank, 2 * cols), 1)
    low = lane < cols

    def fold(x):
        return x + pltpu.roll(x, cols, 1)

    def pack(s):
        hi = s.astype(BF16).astype(F32)
        return jnp.where(low, hi, s - hi).astype(BF16)

    def dot(a, b):
        return lax.dot_general(a, b, (((1,), (0,)), ((), ())), preferred_element_type=F32)

    def dot_t(a, b):
        return lax.dot_general(a, b, (((0,), (0,)), ((), ())), preferred_element_type=F32)

    def up(transfer, left, right):
        return pack(fold(dot_t(transfer, jnp.concatenate([left, right], 0))))

    get_basis.wait()
    skels = []
    half = leaves // 2
    for pair in range(half):
        both = []
        for g in (2 * pair, 2 * pair + 1):
            tile = win_cols[REACH * leaves + g]
            both.append(
                lax.dot_general(
                    basis_v[g],
                    jnp.concatenate([tile, tile], 0),
                    (((1,), (1,)), ((), ())),
                    preferred_element_type=F32,
                )
            )
        win_skel[REACH * half + pair] = jnp.where(low, both[0], both[1]).astype(BF16)
        skels += [pack(s) for s in both]

    def skel_copy(which):
        by = offsets[which]
        return remote(
            win_skel.at[pl.ds(REACH * half, half)],
            win_skel.at[pl.ds((REACH - by) * half, half)],
            skel_send.at[which],
            skel_recv.at[which],
            at(me + by),
        )

    get_local.wait()
    row = 0
    width = half
    current = skels
    while width >= 1:
        current = [
            up(local_v[row + m], current[2 * m], current[2 * m + 1]) for m in range(width)
        ]
        row += width
        width //= 2
    group[cy] = current[0]

    def group_copy(j):
        return remote(
            group.at[cy],
            group.at[cy],
            group_send.at[j],
            group_recv.at[j],
            (cx, lax.rem(cy + j, n_cy)),
        )

    def root_copy(j):
        return remote(
            roots.at[cx],
            roots.at[cx],
            root_send.at[j],
            root_recv.at[j],
            (lax.rem(cx + j, n_cx), cy),
        )

    def group_arrival(j):
        source = lax.rem(cy + n_cy - j, n_cy)
        return remote(
            group.at[source], group.at[source], group_send.at[j], group_recv.at[j], (cx, source)
        )

    def root_arrival(j):
        source = lax.rem(cx + n_cx - j, n_cx)
        return remote(
            roots.at[source], roots.at[source], root_send.at[j], root_recv.at[j], (source, cy)
        )

    for j in range(1, n_cy):
        group_copy(j).start()
    for which, by in enumerate(offsets):

        @pl.when(exists(by))
        def _(which=which):
            skel_copy(which).start()

    for copy in get_upper + get_coup:
        copy.wait()

    def path_term(level, sibling):
        right = lax.rem(lax.div(me, 1 << (level - 1)), 2)
        coupling = coup_v[level - 1].astype(F32)
        turned = jnp.where(right == 1, coupling.T, coupling).astype(BF16)
        return fold(dot(turned, sibling))

    for j in range(1, n_cy):
        group_arrival(j).wait_recv()
    terms = []
    saved = group
    base = 0
    nodes = n_cy
    for level in range(1, up_group + 1):
        nodes //= 2
        for m in range(nodes):
            made = up(
                upper_v[starts[level - 1] + m], saved[base + 2 * m], saved[base + 2 * m + 1]
            )
            if nodes > 1:
                leaf_pairs[(n_cy - 2 * nodes) + m] = made
            else:
                roots[cx] = made
        if nodes > 1:
            saved, base = leaf_pairs, n_cy - 2 * nodes
    for j in range(1, n_cx):
        root_copy(j).start()

    def sibling_at(level):
        mine = lax.div(cy, 1 << (level - 1))
        return mine + 1 - 2 * lax.rem(mine, 2)

    base = 0
    nodes = n_cy
    for level in range(1, up_group + 1):
        if level == 1:
            sibling = group[sibling_at(level)]
        else:
            sibling = leaf_pairs[base + sibling_at(level)]
        terms.append(path_term(level, sibling))
        nodes //= 2
        base = n_cy - 2 * nodes

    get_near.wait()

    def near_dot(tile, block):
        return lax.dot_general(
            tile, block, (((1,), (1,)), ((), ())), preferred_element_type=F32
        )

    def own_near(g, _):
        acc[g] = near_dot(win_cols[REACH * leaves + g], near_v[g, 0])
        return 0

    lax.fori_loop(0, leaves, own_near, 0)

    for j in range(1, n_cx):
        root_arrival(j).wait_recv()

    if n_cx > 1:
        for x in range(n_cx):
            leaf_pairs[n_cy + x] = roots[x]
        base, nodes = n_cy, n_cx
        fresh = n_cy + n_cx
        for level in range(up_group + 1, up_all + 1):
            mine = lax.div(cx, 1 << (level - up_group - 1))
            sibling = leaf_pairs[base + mine + 1 - 2 * lax.rem(mine, 2)]
            terms.append(path_term(level, sibling))
            nodes //= 2
            if nodes > 1:
                for m in range(nodes):
                    leaf_pairs[fresh + m] = up(
                        upper_v[starts[level - 1] + m],
                        leaf_pairs[base + 2 * m],
                        leaf_pairs[base + 2 * m + 1],
                    )
                base = fresh
                fresh += nodes

    coef = terms[-1]
    for level in range(up_all - 1, 0, -1):
        place = lax.div(cy, 1 << level) if level <= up_group else lax.div(me, 1 << level)
        right = lax.rem(lax.div(me, 1 << (level - 1)), 2)
        rows = upper_v[starts[level - 1] + place, pl.ds(pl.multiple_of(right * rank, rank), rank)]
        coef = fold(dot(rows, pack(coef))) + terms[level - 1]
    coefs = [coef]
    width = 1
    row = leaves - 1
    while width < leaves:
        row -= width
        following = []
        for m in range(width):
            made = fold2(dot(local_v[row + m], pack(coefs[m])), cols)
            following += [made[:rank], made[rank:]]
        coefs = following
        width *= 2

    for which, by in enumerate(offsets):

        @pl.when(exists(-by))
        def _(which=which):
            skel_copy(which).wait_recv()

    get_far.wait()
    first = (me - REACH) * leaves

    def slot_of(leaf_id):
        return jnp.clip(leaf_id - first, 0, (2 * REACH + 1) * leaves - 1)

    high_row = (lax.broadcasted_iota(jnp.int32, (1, 2 * cols), 1) >= cols).astype(F32)
    leafcoefs = []
    for g in range(leaves):
        total = None
        for k in range(kfar):
            index = slot_of(far_ids[g, k])
            parity = (index & 1).astype(F32)
            keep = (parity * high_row + (1.0 - parity) * (1.0 - high_row)).astype(BF16)
            term = dot(far_v[g, k], win_skel[index >> 1] * keep)
            total = term if total is None else total + term
        leafcoef = coefs[g] + fold(total)
        coef_half = leafcoef[:, :cols].astype(BF16)
        acc[g] = acc[g] + dot_t(coef_half, basis_v[g])

    relays = jnp.where(odd == 1, me >= 2, me + 2 < n)
    relayed = jnp.where(odd == 1, me + 2 < n, me >= 2)
    for chunk in range(CHUNKS):
        for which, by in enumerate((2, -2)):

            @pl.when(exists(-by))
            def _(which=which, chunk=chunk):
                cols_copy(which, chunk).wait_recv()

        @pl.when(relays)
        def _(chunk=chunk):
            relay_copy(chunk).start()

    mate_copy.wait_recv()
    for chunk in range(CHUNKS):

        @pl.when(relayed)
        def _(chunk=chunk):
            relay_copy(chunk).wait_recv()

    def far_near(g, _):
        total = acc[g]
        for k in range(1, knear):
            total = total + near_dot(win_cols[slot_of(near_ids[g, k])], near_v[g, k])
        out[g] = total.astype(BF16)
        return 0

    lax.fori_loop(0, leaves, far_near, 0)

    for chunk in range(CHUNKS):
        for which, by in enumerate((2, -2)):

            @pl.when(exists(by))
            def _(which=which, chunk=chunk):
                cols_copy(which, chunk).wait_send()

        @pl.when(relays)
        def _(chunk=chunk):
            relay_copy(chunk).wait_send()

    mate_copy.wait_send()
    for which, by in enumerate(offsets):

        @pl.when(exists(by))
        def _(which=which):
            skel_copy(which).wait_send()

    for j in range(1, n_cy):
        group_copy(j).wait_send()
    for j in range(1, n_cx):
        root_copy(j).wait_send()


def fold2(x, cols):
    return x + pltpu.roll(x, cols, 1)


def solution(mesh):
    n_cx, n_cy = mesh.shape["cx"], mesh.shape["cy"]
    n = n_cx * n_cy

    def local(
        points, basis, near, near_ids, local_transfer, far, far_ids, upper_transfer, upper_coupling
    ):
        leaves, cols, leaf = points.shape
        rank = basis.shape[1]
        up_group, up_all = levels_of(n_cy), levels_of(n)
        window = 2 * REACH + 1
        kept = n_cy + n_cx
        any_space = pl.BlockSpec(memory_space=pl.ANY)
        dma = pltpu.SemaphoreType.DMA
        return pl.pallas_call(
            functools.partial(kernel, n_cx, n_cy),
            out_shape=jax.ShapeDtypeStruct(points.shape, points.dtype),
            in_specs=[pl.BlockSpec(memory_space=pltpu.SMEM)] * 2 + [any_space] * 7,
            out_specs=pl.BlockSpec(memory_space=pltpu.VMEM),
            scratch_shapes=[
                pltpu.VMEM((window * leaves, cols, leaf), BF16),
                pltpu.VMEM((window * leaves // 2, rank, 2 * cols), BF16),
                pltpu.VMEM(basis.shape, BF16),
                pltpu.VMEM(near.shape, BF16),
                pltpu.VMEM(local_transfer.shape, BF16),
                pltpu.VMEM(far.shape, BF16),
                pltpu.VMEM((kept,) + upper_transfer.shape[1:], BF16),
                pltpu.VMEM((up_all,) + upper_coupling.shape[1:], BF16),
                pltpu.VMEM((leaves, cols, leaf), F32),
                pltpu.VMEM((n_cy + 2 * n_cx, rank, 2 * cols), BF16),
                pltpu.VMEM((n_cy, rank, 2 * cols), BF16),
                pltpu.VMEM((n_cx, rank, 2 * cols), BF16),
                dma((5 + 2 * up_all,)),
                dma((2, CHUNKS)),
                dma((2, CHUNKS)),
                dma,
                dma,
                dma((CHUNKS,)),
                dma((CHUNKS,)),
                dma((4,)),
                dma((4,)),
                dma((n_cy,)),
                dma((n_cy,)),
                dma((n_cx,)),
                dma((n_cx,)),
            ],
            compiler_params=pltpu.CompilerParams(
                collective_id=0, has_side_effects=True, vmem_limit_bytes=56 * 2**20
            ),
        )(near_ids, far_ids, points, basis, near, local_transfer, far, upper_transfer, upper_coupling)

    split = ("cx", "cy")
    return jax.shard_map(
        local,
        mesh=mesh,
        in_specs=(
            P(split, None, None),
            P(split, None, None),
            P(split, None, None, None),
            P(split, None),
            P(split, None, None),
            P(split, None, None, None),
            P(split, None),
            P(),
            P(),
        ),
        out_specs=P(split, None, None),
        check_vma=False,
    )
```

profile of v0, /device:TPU:1, one launch (start us, length us, event | category | flops | bytes accessed | tf_op | source)
XLA Modules:
  0.0 43.2 jit_solution(1166285021428429184)
XLA Ops:
  0.0 1.3 %copy.10.near_ids = s32[8,4]{1,0:T(8,128)} copy(s32[8,4]{0,1:T(4,128)} %param.12) | data formatting | bytes 256 | tf_op args[3]
  1.3 1.7 %copy.11.local_transfer = bf16[7,128,64]{2,1,0:T(8,128)(2,1)} copy(bf16[7,128,64]{1,2,0:T(8,128)(2,1)} %param.13) | data formatting | bytes 229376 | tf_op args[4]
  3.1 2.4 %copy.12.upper_transfer = bf16[31,128,64]{2,1,0:T(8,128)(2,1)} copy(bf16[31,128,64]{1,2,0:T(8,128)(2,1)} %param.16) | data formatting | bytes 1015808 | tf_op args[7]
  5.4 36.1 %shard_map.91 = bf16[8,64,256]{2,1,0:T(8,128)(2,1)} custom-call(s32[8,4]{1,0:T(8,128)} %copy.10.near_ids, s32[8,8]{1,0:T(8,128)} %far_ids.1, bf16[8,64,256]{2,1,0:T(8,128)(2,1)} %points.1, bf16[8,64,256]{2,1,0:T(8,128)(2,1)} %basis.1, bf16[8,4,256,256]{3,2,1,0:T(8,128)(2,1)} %near.1, bf16[7,128,64]{2,1,0:T(8,128)(2,1)} %copy.11.local_transfer, ...), custom_call_target="tpu_custom_call" | custom-call | tf_op jit(solution)/shard_map/pallas_call | solution.py:482
  41.6 1.7 %copy.14 = bf16[8,64,256]{2,1,0:T(8,128)(2,1)} copy(bf16[8,64,256]{2,1,0:T(8,128)(2,1)} %shard_map.91) | data formatting | bytes 524288
where the time goes:
time: 43.5 us; the launch traced here: 43.2 us
  Pallas kernels  36.1 us (83%)
  local copies, waits for them, and re-layouts  7.09 us (16%)
    pallas_call x1, Pallas kernels, local(): pl.pallas_call(functools.partial(kernel, n_cx, n_cy), out_shape=jax.Shape...  36.1 us
    unnamed x4, local copies, waits for them, and re-layouts  7.09 us

commit v1 on v0

--- a/solution.py
+++ b/solution.py
@@ -9,7 +9,7 @@
 
 F32 = jnp.float32
 BF16 = jnp.bfloat16
-CHUNKS = 2
+CHUNKS = 4
 REACH = 2
 
 
@@ -39,18 +39,21 @@
     upper_v,
     coup_v,
     acc,
+    local_down,
+    path_down,
+    far_sum,
     leaf_pairs,
     group,
     roots,
     load_sem,
-    cols_send,
-    cols_recv,
+    x_send,
+    x_recv,
+    y_send,
+    y_recv,
     mate_send,
     mate_recv,
     relay_send,
     relay_recv,
-    skel_send,
-    skel_recv,
     group_send,
     group_recv,
     root_send,
@@ -120,19 +123,13 @@
         edge = cy < -by if by < 0 else cy + by >= n_cy
         return jnp.logical_and(exists(by), edge)
 
-    offsets = (2, -2, 1, -1)
-    for by in offsets:
+    for by in (4, -4):
 
         @pl.when(outside(by))
         def _(by=by):
             pl.semaphore_signal(
                 barrier, inc=1, device_id=at(me + by), device_id_type=pl.DeviceIdType.MESH
             )
-
-    peers = n_cy - 1 + n_cx - 1
-    for by in offsets:
-        peers = peers + jnp.where(outside(by), 1, 0)
-    pl.semaphore_wait(barrier, peers)
 
     def remote(src, dst, send, recv, target):
         return pltpu.make_async_remote_copy(
@@ -145,47 +142,77 @@
         )
 
     size = leaves // CHUNKS
-
-    def piece(slot, chunk):
-        return win_cols.at[pl.ds(slot * leaves + chunk * size, size)]
-
-    def cols_copy(which, chunk):
-        by = (2, -2)[which]
-        return remote(
-            piece(REACH, chunk),
-            piece(REACH - by, chunk),
-            cols_send.at[which, chunk],
-            cols_recv.at[which, chunk],
-            at(me + by),
-        )
-
-    mate_copy = remote(
-        win_cols.at[own],
-        win_cols.at[pl.ds((REACH - 1 + 2 * odd) * leaves, leaves)],
-        mate_send,
-        mate_recv,
-        at(mate),
-    )
-
-    def relay_copy(chunk):
-        return remote(
-            piece(4 - 4 * odd, chunk),
-            piece(3 - 2 * odd, chunk),
-            relay_send.at[chunk],
-            relay_recv.at[chunk],
+    half = leaves // 2
+    chip_odd = lax.rem(lax.div(me, 2), 2)
+    pair_mate = me + 2 - 4 * chip_odd
+    pair_slot, onward_slot = 4 - 4 * chip_odd, 4 * chip_odd
+    onward = jnp.where(chip_odd == 0, me + 4 < n, me >= 4)
+    incoming = jnp.where(chip_odd == 0, me >= 4, me + 4 < n)
+    relays = jnp.where(odd == 1, me >= 2, me + 2 < n)
+    relayed = jnp.where(odd == 1, me + 2 < n, me >= 2)
+    early = jnp.logical_and(relays, chip_odd == odd)
+    late = jnp.logical_and(relays, chip_odd != odd)
+
+    def unit(slot, u):
+        if u == CHUNKS:
+            return win_skel.at[pl.ds(slot * half, half)]
+        return win_cols.at[pl.ds(slot * leaves + u * size, size)]
+
+    def x_copy(u):
+        return remote(
+            unit(REACH, u), unit(onward_slot, u), x_send.at[u], x_recv.at[u], at(pair_mate)
+        )
+
+    def y_copy(u):
+        return remote(
+            unit(pair_slot, u),
+            unit(onward_slot, u),
+            y_send.at[u],
+            y_recv.at[u],
+            at(me + 4 - 8 * chip_odd),
+        )
+
+    def relay_copy(u):
+        return remote(
+            unit(4 - 4 * odd, u), unit(3 - 2 * odd, u), relay_send.at[u], relay_recv.at[u], at(mate)
+        )
+
+    def mate_copy(whole, index):
+        count = whole.shape[0] // (2 * REACH + 1)
+        return remote(
+            whole.at[pl.ds(REACH * count, count)],
+            whole.at[pl.ds((REACH - 1 + 2 * odd) * count, count)],
+            mate_send.at[index],
+            mate_recv.at[index],
             at(mate),
         )
 
+    def forward(u):
+        x_copy(u).wait_recv()
+
+        @pl.when(onward)
+        def _():
+            y_copy(u).start()
+
+        @pl.when(early)
+        def _():
+            relay_copy(u).start()
+
+    def finish(u):
+        @pl.when(incoming)
+        def _():
+            y_copy(u).wait_recv()
+
+        @pl.when(late)
+        def _():
+            relay_copy(u).start()
+
+    def last(u):
+        @pl.when(relayed)
+        def _():
+            relay_copy(u).wait_recv()
+
     get_points.wait()
-    for chunk in range(CHUNKS):
-        for which, by in enumerate((2, -2)):
-
-            @pl.when(exists(by))
-            def _(which=which, chunk=chunk):
-                cols_copy(which, chunk).start()
-
-    mate_copy.start()
-
     lane = lax.broadcasted_iota(jnp.int32, (rank, 2 * cols), 1)
     low = lane < cols
 
@@ -203,11 +230,10 @@
         return lax.dot_general(a, b, (((0,), (0,)), ((), ())), preferred_element_type=F32)
 
     def up(transfer, left, right):
-        return pack(fold(dot_t(transfer, jnp.concatenate([left, right], 0))))
+        return pack(fold(dot(transfer, jnp.concatenate([left, right], 0))))
 
     get_basis.wait()
     skels = []
-    half = leaves // 2
     for pair in range(half):
         both = []
         for g in (2 * pair, 2 * pair + 1):
@@ -223,16 +249,6 @@
         win_skel[REACH * half + pair] = jnp.where(low, both[0], both[1]).astype(BF16)
         skels += [pack(s) for s in both]
 
-    def skel_copy(which):
-        by = offsets[which]
-        return remote(
-            win_skel.at[pl.ds(REACH * half, half)],
-            win_skel.at[pl.ds((REACH - by) * half, half)],
-            skel_send.at[which],
-            skel_recv.at[which],
-            at(me + by),
-        )
-
     get_local.wait()
     row = 0
     width = half
@@ -275,13 +291,17 @@
             roots.at[source], roots.at[source], root_send.at[j], root_recv.at[j], (source, cy)
         )
 
+    peers = n_cy - 1 + n_cx - 1
+    for by in (4, -4):
+        peers = peers + jnp.where(outside(by), 1, 0)
+    pl.semaphore_wait(barrier, peers)
     for j in range(1, n_cy):
         group_copy(j).start()
-    for which, by in enumerate(offsets):
-
-        @pl.when(exists(by))
-        def _(which=which):
-            skel_copy(which).start()
+    x_copy(CHUNKS).start()
+    mate_copy(win_skel, 1).start()
+    for u in range(CHUNKS):
+        x_copy(u).start()
+    mate_copy(win_cols, 0).start()
 
     for copy in get_upper + get_coup:
         copy.wait()
@@ -292,8 +312,15 @@
         turned = jnp.where(right == 1, coupling.T, coupling).astype(BF16)
         return fold(dot(turned, sibling))
 
+    for node in range(leaves - 1):
+        local_down[node] = local_v[node].astype(F32).T.astype(BF16)
+    for level in range(1, up_all):
+        place = lax.div(cy, 1 << level) if level <= up_group else lax.div(me, 1 << level)
+        path_down[level - 1] = upper_v[starts[level - 1] + place].astype(F32).T.astype(BF16)
+
     for j in range(1, n_cy):
         group_arrival(j).wait_recv()
+    forward(CHUNKS)
     terms = []
     saved = group
     base = 0
@@ -313,6 +340,7 @@
     for j in range(1, n_cx):
         root_copy(j).start()
 
+    forward(0)
     def sibling_at(level):
         mine = lax.div(cy, 1 << (level - 1))
         return mine + 1 - 2 * lax.rem(mine, 2)
@@ -340,6 +368,32 @@
         return 0
 
     lax.fori_loop(0, leaves, own_near, 0)
+
+    for u in range(1, CHUNKS - 1):
+        forward(u)
+    finish(CHUNKS)
+    mate_copy(win_skel, 1).wait_recv()
+    last(CHUNKS)
+    get_far.wait()
+    first = (me - REACH) * leaves
+
+    def slot_of(leaf_id):
+        return jnp.clip(leaf_id - first, 0, (2 * REACH + 1) * leaves - 1)
+
+    high_row = (lax.broadcasted_iota(jnp.int32, (1, 2 * cols), 1) >= cols).astype(F32)
+    for g in range(leaves):
+        total = None
+        for k in range(kfar):
+            index = slot_of(far_ids[g, k])
+            parity = (index & 1).astype(F32)
+            keep = (parity * high_row + (1.0 - parity) * (1.0 - high_row)).astype(BF16)
+            term = dot(far_v[g, k], win_skel[index >> 1] * keep)
+            total = term if total is None else total + term
+        far_sum[g] = total
+
+    forward(CHUNKS - 1)
+    for u in range(CHUNKS - 2):
+        finish(u)
 
     for j in range(1, n_cx):
         root_arrival(j).wait_recv()
@@ -366,9 +420,8 @@
 
     coef = terms[-1]
     for level in range(up_all - 1, 0, -1):
-        place = lax.div(cy, 1 << level) if level <= up_group else lax.div(me, 1 << level)
         right = lax.rem(lax.div(me, 1 << (level - 1)), 2)
-        rows = upper_v[starts[level - 1] + place, pl.ds(pl.multiple_of(right * rank, rank), rank)]
+        rows = path_down[level - 1, pl.ds(pl.multiple_of(right * rank, rank), rank)]
         coef = fold(dot(rows, pack(coef))) + terms[level - 1]
     coefs = [coef]
     width = 1
@@ -377,84 +430,43 @@
         row -= width
         following = []
         for m in range(width):
-            made = fold2(dot(local_v[row + m], pack(coefs[m])), cols)
+            made = fold2(dot(local_down[row + m], pack(coefs[m])), cols)
             following += [made[:rank], made[rank:]]
         coefs = following
         width *= 2
 
-    for which, by in enumerate(offsets):
-
-        @pl.when(exists(-by))
-        def _(which=which):
-            skel_copy(which).wait_recv()
-
-    get_far.wait()
-    first = (me - REACH) * leaves
-
-    def slot_of(leaf_id):
-        return jnp.clip(leaf_id - first, 0, (2 * REACH + 1) * leaves - 1)
-
-    high_row = (lax.broadcasted_iota(jnp.int32, (1, 2 * cols), 1) >= cols).astype(F32)
-    leafcoefs = []
     for g in range(leaves):
-        total = None
-        for k in range(kfar):
-            index = slot_of(far_ids[g, k])
-            parity = (index & 1).astype(F32)
-            keep = (parity * high_row + (1.0 - parity) * (1.0 - high_row)).astype(BF16)
-            term = dot(far_v[g, k], win_skel[index >> 1] * keep)
-            total = term if total is None else total + term
-        leafcoef = coefs[g] + fold(total)
-        coef_half = leafcoef[:, :cols].astype(BF16)
+        coef_half = (coefs[g] + fold(far_sum[g]))[:, :cols].astype(BF16)
         acc[g] = acc[g] + dot_t(coef_half, basis_v[g])
 
-    relays = jnp.where(odd == 1, me >= 2, me + 2 < n)
-    relayed = jnp.where(odd == 1, me + 2 < n, me >= 2)
-    for chunk in range(CHUNKS):
-        for which, by in enumerate((2, -2)):
-
-            @pl.when(exists(-by))
-            def _(which=which, chunk=chunk):
-                cols_copy(which, chunk).wait_recv()
-
-        @pl.when(relays)
-        def _(chunk=chunk):
-            relay_copy(chunk).start()
-
-    mate_copy.wait_recv()
-    for chunk in range(CHUNKS):
-
-        @pl.when(relayed)
-        def _(chunk=chunk):
-            relay_copy(chunk).wait_recv()
+    for u in range(CHUNKS - 2, CHUNKS):
+        finish(u)
+    mate_copy(win_cols, 0).wait_recv()
+    for u in range(CHUNKS):
+        last(u)
 
     def far_near(g, _):
         total = acc[g]
         for k in range(1, knear):
-            total = total + near_dot(win_cols[slot_of(near_ids[g, k])], near_v[g, k])
+            total = total + near_dot(win_cols[slot_of(near_ids[k, g])], near_v[g, k])
         out[g] = total.astype(BF16)
         return 0
 
     lax.fori_loop(0, leaves, far_near, 0)
 
-    for chunk in range(CHUNKS):
-        for which, by in enumerate((2, -2)):
-
-            @pl.when(exists(by))
-            def _(which=which, chunk=chunk):
-                cols_copy(which, chunk).wait_send()
+    for u in range(CHUNKS + 1):
+        x_copy(u).wait_send()
+
+        @pl.when(onward)
+        def _(u=u):
+            y_copy(u).wait_send()
 
         @pl.when(relays)
-        def _(chunk=chunk):
-            relay_copy(chunk).wait_send()
-
-    mate_copy.wait_send()
-    for which, by in enumerate(offsets):
-
-        @pl.when(exists(by))
-        def _(which=which):
-            skel_copy(which).wait_send()
-
+        def _(u=u):
+            relay_copy(u).wait_send()
+
+    mate_copy(win_skel, 1).wait_send()
+    mate_copy(win_cols, 0).wait_send()
     for j in range(1, n_cy):
         group_copy(j).wait_send()
     for j in range(1, n_cx):
@@ -474,6 +486,8 @@
     ):
         leaves, cols, leaf = points.shape
         rank = basis.shape[1]
+        local_turned = jnp.swapaxes(local_transfer, 1, 2)
+        upper_turned = jnp.swapaxes(upper_transfer, 1, 2)
         up_group, up_all = levels_of(n_cy), levels_of(n)
         window = 2 * REACH + 1
         kept = n_cy + n_cx
@@ -489,23 +503,26 @@
                 pltpu.VMEM((window * leaves // 2, rank, 2 * cols), BF16),
                 pltpu.VMEM(basis.shape, BF16),
                 pltpu.VMEM(near.shape, BF16),
-                pltpu.VMEM(local_transfer.shape, BF16),
+                pltpu.VMEM(local_turned.shape, BF16),
                 pltpu.VMEM(far.shape, BF16),
-                pltpu.VMEM((kept,) + upper_transfer.shape[1:], BF16),
+                pltpu.VMEM((kept,) + upper_turned.shape[1:], BF16),
                 pltpu.VMEM((up_all,) + upper_coupling.shape[1:], BF16),
                 pltpu.VMEM((leaves, cols, leaf), F32),
+                pltpu.VMEM(local_transfer.shape, BF16),
+                pltpu.VMEM((up_all,) + upper_transfer.shape[1:], BF16),
+                pltpu.VMEM((leaves, rank, 2 * cols), F32),
                 pltpu.VMEM((n_cy + 2 * n_cx, rank, 2 * cols), BF16),
                 pltpu.VMEM((n_cy, rank, 2 * cols), BF16),
                 pltpu.VMEM((n_cx, rank, 2 * cols), BF16),
                 dma((5 + 2 * up_all,)),
-                dma((2, CHUNKS)),
-                dma((2, CHUNKS)),
-                dma,
-                dma,
-                dma((CHUNKS,)),
-                dma((CHUNKS,)),
-                dma((4,)),
-                dma((4,)),
+                dma((CHUNKS + 1,)),
+                dma((CHUNKS + 1,)),
+                dma((CHUNKS + 1,)),
+                dma((CHUNKS + 1,)),
+                dma((2,)),
+                dma((2,)),
+                dma((CHUNKS + 1,)),
+                dma((CHUNKS + 1,)),
                 dma((n_cy,)),
                 dma((n_cy,)),
                 dma((n_cx,)),
@@ -514,7 +531,7 @@
             compiler_params=pltpu.CompilerParams(
                 collective_id=0, has_side_effects=True, vmem_limit_bytes=56 * 2**20
             ),
-        )(near_ids, far_ids, points, basis, near, local_transfer, far, upper_transfer, upper_coupling)
+        )(near_ids.T, far_ids, points, basis, near, local_turned, far, upper_turned, upper_coupling)
 
     split = ("cx", "cy")
     return jax.shard_map(

time: 43.5 us -> 25.6 us (0.59)
  the two profiles are of different devices: /device:TPU:1 before, /device:TPU:8 now
where the time goes in v1:
time: 25.6 us; the launch traced here: 25.4 us
  Pallas kernels  23.7 us (93%)
  local copies, waits for them, and re-layouts  1.67 us (7%)
    pallas_call x1, Pallas kernels, local(): pl.pallas_call(functools.partial(kernel, n_cx, n_cy), out_shape=jax.Shape...  23.7 us
    unnamed x1, local copies, waits for them, and re-layouts  1.67 us

profile of v1, /device:TPU:8, one launch (start us, length us, event | category | flops | bytes accessed | tf_op | source)
XLA Modules:
  0.0 25.4 jit_solution(11805014453374453695)
XLA Ops:
  0.0 23.7 %shard_map.91 = bf16[8,64,256]{2,1,0:T(8,128)(2,1)} custom-call(s32[4,8]{1,0:T(4,128)} %bitcast.5, s32[8,8]{1,0:T(8,128)} %far_ids.1, bf16[8,64,256]{2,1,0:T(8,128)(2,1)} %points.1, bf16[8,64,256]{2,1,0:T(8,128)(2,1)} %basis.1, bf16[8,4,256,256]{3,2,1,0:T(8,128)(2,1)} %near.1, bf16[7,64,128]{2,1,0:T(8,128)(2,1)} %bitcast.4, bf16[8,8,64,64]{3,2,1,0:T(8,128)(2,1)} %far.1, ...), custom_call_target="tpu_custom_call" | custom-call | tf_op jit(solution)/shard_map/pallas_call | solution.py:496
  23.7 1.7 %copy.11 = bf16[8,64,256]{2,1,0:T(8,128)(2,1)} copy(bf16[8,64,256]{2,1,0:T(8,128)(2,1)} %shard_map.91) | data formatting | bytes 524288
